TPU v7x, 256 devices: a whole 4x4x8 slice. The times are simulated.
256 devices in a mesh: rows: 4 (over x), chan: 8 (over y, z_lo), filt: 8 (over z_hi, core).
Axes of the slice: x: 4, y: 4, z: 8 (z_hi: 4, z_lo: 2; z = z_hi * 2 + z_lo), core: 2. Of those that a mesh axis runs over, the one named last changes fastest.
Arguments:
- images: bfloat16 [16, 2048, 2048], P('rows', 'chan', 'filt'), may hold values from -6 to 6
- first_weight: bfloat16 [2048, 1024], P('chan', 'filt'), may hold values from -0.125 to 0.125
- group_weight: bfloat16 [3, 3, 32, 1024], P(None, None, None, 'filt'), may hold values from -0.375 to 0.375
- third_weight: bfloat16 [1024, 2048], P('chan', 'filt'), may hold values from -0.1875 to 0.1875
- out_grad: bfloat16 [16, 2048, 2048], P('rows', 'chan', 'filt'), may hold values from -6 to 6
Outputs:
- block_out: bfloat16 [16, 2048, 2048], P('rows', 'chan', 'filt')
- images_grad: float32 [16, 2048, 2048], P('rows', 'chan', 'filt')
- first_grad: float32 [2048, 1024], P('chan', 'filt')
- group_grad: float32 [3, 3, 32, 1024], P(None, None, None, 'filt')
- third_grad: float32 [1024, 2048], P('chan', 'filt')
All inputs are finite; a program needn't handle non-finite values.
Results may differ from a plain program's by a relative error of at most 0.006.
Values may be sent and summed in bfloat16 or wider, within the bound.
No kernel may reach another device: no remote copies, remote signals or barrier semaphores. Data moves between devices by JAX's collectives and lax.ppermute only.
A program may use at most 128 MiB of HBM per device.

v0:
```python
import jax
import jax.numpy as jnp
from jax import lax
from jax.sharding import PartitionSpec as P


def extended(block, sides, width):
    for axis, dim in sides:
        count = lax.axis_size(axis)
        forward = [(i, i + 1) for i in range(count - 1)]
        backward = [(target, source) for source, target in forward]
        low = lax.ppermute(
            lax.slice_in_dim(block, block.shape[dim] - width, None, axis=dim), axis, forward
        )
        high = lax.ppermute(lax.slice_in_dim(block, 0, width, axis=dim), axis, backward)
        block = jnp.concatenate([low, block, high], axis=dim)
    return block


def silu_slope(values):
    logistic = jax.nn.sigmoid(values)
    return logistic * (1.0 + values * (1.0 - logistic))


def group_conv(padded, kernel, groups_here):
    result = lax.conv_general_dilated(
        padded[None],
        kernel,
        (1, 1),
        "VALID",
        dimension_numbers=("NHWC", "HWIO", "NHWC"),
        feature_group_count=groups_here,
        preferred_element_type=jnp.float32,
    )
    return result[0]


def transposed_kernel(kernel, group_size, groups_here):
    pieces = kernel.reshape(3, 3, group_size, groups_here, group_size)
    swapped = jnp.transpose(pieces, (0, 1, 4, 3, 2)).reshape(
        3, 3, group_size, groups_here * group_size
    )
    return swapped[::-1, ::-1]


def kernel_partial(padded_first, group_delta, group_size, groups_here):
    rows_here = group_delta.shape[0]
    cols_here = group_delta.shape[1]
    pixels = rows_here * cols_here
    delta_groups = group_delta.reshape(pixels, groups_here, group_size)
    kernel_terms = []
    for row_shift in range(3):
        for col_shift in range(3):
            window = padded_first[
                row_shift : row_shift + rows_here, col_shift : col_shift + cols_here
            ]
            window = window.reshape(pixels, groups_here, group_size)
            kernel_terms.append(
                jnp.einsum("pgi,pgo->gio", window, delta_groups, preferred_element_type=jnp.float32)
            )
    kernel_part = jnp.stack(kernel_terms).reshape(3, 3, groups_here, group_size, group_size)
    kernel_part = jnp.transpose(kernel_part, (0, 1, 3, 2, 4))
    return kernel_part.reshape(3, 3, group_size, groups_here * group_size)


def body(images, first_weight, group_weight, third_weight, out_grad):
    rows_here = images.shape[0]
    cols_here = images.shape[1]
    group_size = group_weight.shape[2]
    first_panel, third_panel = (
        lax.all_gather(first_weight, "chan", axis=0, tiled=True),
        lax.all_gather(third_weight, "chan", axis=0, tiled=True),
    )
    pixels = rows_here * cols_here
    groups_here = group_weight.shape[3] // group_size
    gathered = lax.all_gather(images, "filt", axis=2, tiled=True)
    flat_images = gathered.reshape(pixels, gathered.shape[2])
    pre_first = jnp.dot(flat_images, first_panel, preferred_element_type=jnp.float32)
    act_first = (
        jax.nn.silu(pre_first)
        .astype(jnp.bfloat16)
        .reshape(rows_here, cols_here, first_panel.shape[1])
    )
    padded_first = extended(act_first, (("rows", 0), ("chan", 1)), 1)
    pre_group = group_conv(padded_first, group_weight, groups_here)
    act_group = jax.nn.silu(pre_group).astype(jnp.bfloat16)
    mid_whole = lax.all_gather(act_group, "filt", axis=2, tiled=True)
    flat_mid = mid_whole.reshape(pixels, mid_whole.shape[2])
    third_out = jnp.dot(flat_mid, third_panel, preferred_element_type=jnp.float32)
    own_images = images.reshape(pixels, images.shape[2]).astype(jnp.float32)
    block_out = (own_images + third_out).astype(jnp.bfloat16).reshape(images.shape)
    grad_flat = out_grad.reshape(pixels, out_grad.shape[2])
    mid_terms = lax.dot_general(
        grad_flat, third_panel, (((1,), (1,)), ((), ())), preferred_element_type=jnp.float32
    )
    mid_grad = lax.psum_scatter(
        mid_terms.reshape(rows_here, cols_here, mid_terms.shape[1]),
        "filt",
        scatter_dimension=2,
        tiled=True,
    )
    third_part = lax.dot_general(
        flat_mid, grad_flat, (((0,), (0,)), ((), ())), preferred_element_type=jnp.float32
    )
    group_delta = (mid_grad * silu_slope(pre_group)).astype(jnp.bfloat16)
    padded_delta = extended(group_delta, (("rows", 0), ("chan", 1)), 1)
    first_back = group_conv(
        padded_delta, transposed_kernel(group_weight, group_size, groups_here), groups_here
    )
    kernel_part = kernel_partial(padded_first, group_delta, group_size, groups_here)
    first_delta = (first_back.reshape(pixels, first_back.shape[2]) * silu_slope(pre_first)).astype(
        jnp.bfloat16
    )
    first_part = lax.dot_general(
        flat_images, first_delta, (((0,), (0,)), ((), ())), preferred_element_type=jnp.float32
    )
    input_terms = lax.dot_general(
        first_delta, first_panel, (((1,), (1,)), ((), ())), preferred_element_type=jnp.float32
    )
    back_images = lax.psum_scatter(
        input_terms.reshape(rows_here, cols_here, input_terms.shape[1]).astype(jnp.bfloat16),
        "filt",
        scatter_dimension=2,
        tiled=True,
    ).astype(jnp.float32)
    images_grad = out_grad.astype(jnp.float32) + back_images
    group_grad = lax.psum(kernel_part, ("rows", "chan"))
    first_total, third_total = lax.psum((first_part, third_part), "rows")
    first_grad, third_grad = (
        lax.psum_scatter(first_total, "chan", scatter_dimension=0, tiled=True),
        lax.psum_scatter(third_total, "chan", scatter_dimension=0, tiled=True),
    )
    return (block_out, images_grad, first_grad, group_grad, third_grad)


def solution(mesh):
    in_specs = (
        P("rows", "chan", "filt"),
        P("chan", "filt"),
        P(None, None, None, "filt"),
        P("chan", "filt"),
        P("rows", "chan", "filt"),
    )
    out_specs = (
        P("rows", "chan", "filt"),
        P("rows", "chan", "filt"),
        P("chan", "filt"),
        P(None, None, None, "filt"),
        P("chan", "filt"),
    )
    return jax.shard_map(body, mesh=mesh, in_specs=in_specs, out_specs=out_specs, check_vma=False)
```

profile of v0, /device:TPU:32, one launch (start us, length us, event | category | flops | bytes accessed | tf_op | source)
XLA Modules:
  0.0 700.0 jit_solution(2654013649618200023)
XLA Ops:
  7.9 39.6 %all_gather.15 = bf16[1024,256]{1,0:T(8,128)(2,1)S(1)} all-gather(bf16[128,256]{1,0:T(8,128)(2,1)} %param.8), channel_id=1, replica_groups=mesh['rows'=4,'chan'=8,'filt'=8] {'chan'}, dimensions={0}, use_global_device_ids=true | all-gather | bytes 589824 | tf_op jit(solution)/shard_map/all_gather | solution.py:72
  47.5 3.8 fusion.10
  52.2 36.9 %all_gather.13 = bf16[2048,128]{1,0:T(8,128)(2,1)S(1)} all-gather(bf16[256,128]{1,0:T(8,128)(2,1)S(1)} %copy-done.13), channel_id=1, replica_groups=mesh['rows'=4,'chan'=8,'filt'=8] {'chan'}, dimensions={0}, use_global_device_ids=true | all-gather | bytes 589824 | tf_op jit(solution)/shard_map/all_gather | solution.py:71
  89.1 4.4 multiply_convert_fusion.3
  93.5 2.9 collective-permute-start
  96.4 1.3 collective-permute-start.1
  98.4 4.2 collective-permute-done.1
  103.2 3.4 collective-permute-start.2
  106.6 3.2 collective-permute-start.3
  110.7 8.0 %collective-permute-done.2 = bf16[6,1,128]{1,2,0:T(8,128)(2,1)S(1)} collective-permute-done((bf16[6,1,128]{1,2,0:T(8,128)(2,1)S(1)}, bf16[6,1,128]{1,2,0:T(8,128)(2,1)S(1)}, u32[]{:S(2)}, u32[]{:S(2)}) %collective-permute-start.2) | collective-permute-done | bytes 1568 | tf_op jit(solution)/shard_map/ppermute | solution.py:12
  118.7 10.6 %collective-permute-done.3 = bf16[6,1,128]{1,2,0:T(8,128)(2,1)S(1)} collective-permute-done((bf16[6,1,128]{1,2,0:T(8,128)(2,1)S(1)}, bf16[6,1,128]{1,2,0:T(8,128)(2,1)S(1)}, u32[]{:S(2)}, u32[]{:S(2)}) %collective-permute-start.3) | collective-permute-done | bytes 1568 | tf_op jit(solution)/shard_map/ppermute | solution.py:15
  130.0 5.8 copy.36
  135.8 9.4 %fusion.13 = f32[1,4,256,4,32]{4,0,3,2,1:T(1,128)S(1)} fusion(bf16[1,6,258,4,32]{4,0,3,2,1:T(2,128)(2,1)} %copy.36, bf16[3,3,32,4,32]{4,3,2,1,0:T(4,128)(2,1)} %shard_map.94), kind=kOutput, calls=%fused_computation.39 | convolution fusion | flops 75497472 | bytes 994304 | tf_op jit(solution)/shard_map/conv_general_dilated | solution.py:26
  145.3 3.5 copy.38
  148.8 1.3 copy.40
  150.2 2.0 multiply_convert_fusion.1
  152.2 3.3 collective-permute-start.4
  155.6 1.3 collective-permute-start.5
  157.5 4.3 collective-permute-done.5
  161.8 3.5 collective-permute-start.6
  165.3 2.6 collective-permute-start.7
  169.2 2.5 collective-permute-done.7
  172.1 5.9 copy.44
  178.0 13.8 %convolution_reduce_fusion = f32[4,256,4,32]{3,2,1,0:T(4,128)S(1)} fusion(bf16[1,6,258,4,32]{4,0,3,2,1:T(2,128)(2,1)} %copy.44, bf16[3,3,32,4,32]{4,3,2,1,0:T(4,128)(2,1)} %rev.6), kind=kOutput, calls=%fused_computation.2 | convolution fusion | flops 75497472 | bytes 994304 | tf_op jit(solution)/shard_map/conv_general_dilated | solution.py:26
  191.8 1.7 reshape.99
  193.5 1.4 multiply_convert_fusion
  194.9 4.0 convolution_bitcast_fusion
  199.0 3.4 convolution_bitcast_fusion.1
  202.4 40.0 %reduce-scatter.9.cloned.1.call-done = f32[256,128]{0,1:T(8,128)} async-done(((f32[2048,128]{0,1:T(8,128)}), f32[256,128]{0,1:T(8,128)}) %reduce-scatter.9.cloned.1.call-update) | async-done | bytes 131088 | tf_op jit(solution)/shard_map/reduce_scatter | solution.py:130
  242.4 44.5 %reduce-scatter.11.cloned.1.call-done = f32[128,256]{1,0:T(8,128)} async-done(((f32[1024,256]{1,0:T(8,128)}), f32[128,256]{1,0:T(8,128)}) %reduce-scatter.11.cloned.1.call-update) | async-done | bytes 131088 | tf_op jit(solution)/shard_map/reduce_scatter | solution.py:131
  286.9 3.2 convolution_convert_fusion
  291.8 1.2 pad_maximum_fusion.1
  294.3 1.8 reshape.85
  297.0 1.1 reshape.88
  299.1 1.8 reshape.89
  302.2 1.1 reshape.91
  304.2 1.1 reshape.93
  306.2 1.1 reshape.86
  307.3 1.1 fusion.9
  308.9 1.2 fusion.6
  311.5 0.9 reshape.95
  312.5 3.2 fusion
  315.6 21.3 %all-reduce.6.cloned.1.call-done = (f32[256,128]{0,1:T(8,128)}, f32[128,256]{1,0:T(8,128)}) async-done(((f32[256,128]{0,1:T(8,128)}, f32[128,256]{1,0:T(8,128)}), (f32[256,128]{0,1:T(8,128)}, f32[128,256]{1,0:T(8,128)})) %all-reduce.6.cloned.1.call-update) | async-done | bytes 262160 | tf_op jit(solution)/shard_map/psum | solution.py:128
  337.0 1.7 copy.60
  338.7 59.3 %reduce-scatter.7.cloned.1.call-done = bf16[4,256,256]{2,1,0:T(8,128)(2,1)} async-done(((bf16[4,256,2048]{2,1,0:T(8,128)(2,1)}), bf16[4,256,256]{2,1,0:T(8,128)(2,1)}) %reduce-scatter.7.cloned.1.call-update) | async-done | bytes 524304 | tf_op jit(solution)/shard_map/reduce_scatter | solution.py:120
  398.0 2.1 convert_add_fusion
  400.1 290.7 %all-reduce.4.cloned.1.call-done = f32[3,3,32,128]{3,2,1,0:T(8,128)} async-done(((f32[3,3,32,128]{3,2,1,0:T(8,128)}), f32[3,3,32,128]{3,2,1,0:T(8,128)}) %all-reduce.4.cloned.1.call-update) | async-done | bytes 147472 | tf_op jit(solution)/shard_map/psum | solution.py:127
  690.9 1.6 copy.78
  (90 shorter events, 17.4 us)
Async XLA Ops:
  7.2 81.9 %all-gather.3.cloned.1.call-start = ((), (), s32[]{:S(2)}) async-start(), calls=%async_computation.4 | async-start | bytes 4718592 | tf_op jit(solution)/shard_map/all_gather | solution.py:76
  7.9 142.2 %reduce-scatter.5.cloned.1.call-start = ((), (), s32[]{:S(2)}) async-start(), calls=%async_computation.6 | async-start | bytes 4718592 | tf_op jit(solution)/shard_map/reduce_scatter | solution.py:96
  51.3 0.8 copy-start.13
  51.4 147.6 %all-gather.5.cloned.1.call-start = ((), (), s32[]{:S(2)}) async-start(), calls=%async_computation.5 | async-start | bytes 2359296 | tf_op jit(solution)/shard_map/all_gather | solution.py:87
  89.1 4.4 copy-start
  93.5 16.3 %copy-start.12 = (bf16[3,3,32,128]{3,2,1,0:T(8,128)(2,1)S(1)}, bf16[3,3,32,128]{3,2,1,0:T(8,128)(2,1)}, u32[]{:S(2)}) copy-start(bf16[3,3,32,128]{3,2,1,0:T(8,128)(2,1)} %param.7) | copy-start | bytes 221188
  93.5 4.8 collective-permute-start
  96.4 6.2 collective-permute-start.1
  98.3 4.6 copy-start.7
  102.6 0.6 copy-start.9
  103.2 15.5 %collective-permute-start.2 = (bf16[6,1,128]{1,2,0:T(8,128)(2,1)S(1)}, bf16[6,1,128]{1,2,0:T(8,128)(2,1)S(1)}, u32[]{:S(2)}, u32[]{:S(2)}) collective-permute-start(bf16[6,1,128]{1,2,0:T(8,128)(2,1)S(1)} %get-tuple-element.29), channel_id=1, source_target_pairs={{0,8},{8,16},{16,24},{24,32},{32,40},{40,48},{48,56},{1,9},{9,17},... | collective-permute-start | bytes 4616 | tf_op jit(solution)/shard_map/ppermute | solution.py:12
  106.6 22.7 %collective-permute-start.3 = (bf16[6,1,128]{1,2,0:T(8,128)(2,1)S(1)}, bf16[6,1,128]{1,2,0:T(8,128)(2,1)S(1)}, u32[]{:S(2)}, u32[]{:S(2)}) collective-permute-start(bf16[6,1,128]{1,2,0:T(8,128)(2,1)S(1)} %get-tuple-element.30), channel_id=1, source_target_pairs={{8,0},{16,8},{24,16},{32,24},{40,32},{48,40},{56,48},{9,1},{17,9},... | collective-permute-start | bytes 4616 | tf_op jit(solution)/shard_map/ppermute | solution.py:15
  118.7 17.1 %copy-start.4 = (bf16[6,1,128]{1,2,0:T(8,128)(2,1)}, bf16[6,1,128]{1,2,0:T(8,128)(2,1)S(1)}, u32[]{:S(2)}) copy-start(bf16[6,1,128]{1,2,0:T(8,128)(2,1)S(1)} %collective-permute-done.2) | copy-start | bytes 4612
  129.3 0.7 copy-start.6
  148.8 19.0 %copy-start.3 = (bf16[3,3,32,4,32]{4,3,2,1,0:T(4,128)(2,1)S(1)}, bf16[3,3,32,4,32]{4,3,2,1,0:T(4,128)(2,1)}, u32[]{:S(2)}) copy-start(bf16[3,3,32,4,32]{4,3,2,1,0:T(4,128)(2,1)} %shard_map.94) | copy-start | bytes 221188
  152.2 90.2 %reduce-scatter.9.cloned.1.call-start = ((), (), s32[]{:S(2)}) async-start(), calls=%async_computation.9 | async-start | bytes 1179648 | tf_op jit(solution)/shard_map/reduce_scatter | solution.py:130
  152.2 5.2 collective-permute-start.4
  155.6 6.2 collective-permute-start.5
  161.8 7.4 %collective-permute-start.6 = (bf16[6,1,128]{2,1,0:T(2,128)(2,1)S(1)}, bf16[6,1,128]{2,1,0:T(2,128)(2,1)S(1)}, u32[]{:S(2)}, u32[]{:S(2)}) collective-permute-start(bf16[6,1,128]{2,1,0:T(2,128)(2,1)S(1)} %get-tuple-element.27), channel_id=1, source_target_pairs={{0,8},{8,16},{16,24},{24,32},{32,40},{40,48},{48,56},{1,9},{9,17},... | collective-permute-start | bytes 4616 | tf_op jit(solution)/shard_map/ppermute | solution.py:12
  165.3 6.4 collective-permute-start.7
  194.9 4.1 copy-start.2
  198.9 88.0 %copy-start.1 = (bf16[2048,128]{1,0:T(8,128)(2,1)S(1)}, bf16[2048,128]{1,0:T(8,128)(2,1)}, u32[]{:S(2)}) copy-start(bf16[2048,128]{1,0:T(8,128)(2,1)} %copy-done) | copy-start | bytes 1572868
  198.9 88.0 %reduce-scatter.11.cloned.1.call-start = ((), (), s32[]{:S(2)}) async-start(), calls=%async_computation.10 | async-start | bytes 1179648 | tf_op jit(solution)/shard_map/reduce_scatter | solution.py:131
  202.4 134.6 %all-reduce.6.cloned.1.call-start = ((), (), s32[]{:S(2)}) async-start(), calls=%async_computation.11 | async-start | bytes 524288 | tf_op jit(solution)/shard_map/psum | solution.py:128
  286.9 111.1 %reduce-scatter.7.cloned.1.call-start = ((), (), s32[]{:S(2)}) async-start(), calls=%async_computation.7 | async-start | bytes 4718592 | tf_op jit(solution)/shard_map/reduce_scatter | solution.py:120
  290.2 0.8 copy-start.8
  290.2 0.9 copy-start.10
  290.2 1.6 copy-start.5
  290.2 400.7 %all-reduce.4.cloned.1.call-start = ((), (), s32[]{:S(2)}) async-start(), calls=%async_computation.8 | async-start | bytes 294912 | tf_op jit(solution)/shard_map/psum | solution.py:127
  337.0 355.5 %copy-start.11 = (f32[128,256]{1,0:T(8,128)S(1)}, f32[128,256]{1,0:T(8,128)}, u32[]{:S(2)}) copy-start(f32[128,256]{1,0:T(8,128)} %get-tuple-element.46) | copy-start | bytes 393220
Sparse Core Ops, SparseCore 0:
  9.8 60.3 all-gather.2
  72.7 76.7 reduce-scatter.4
  152.3 42.8 all-gather.4
  199.0 43.3 reduce-scatter.8
  244.8 42.0 reduce-scatter.10
  289.1 47.8 all-reduce.5
  339.7 58.2 reduce-scatter.6
  401.4 289.4 all-reduce.3
where the time goes:
time: 701 us; the launch traced here: 700 us
  waiting for transfers between devices  487 us (69%)
  blocking collectives  76.5 us (11%)
  matrix products  49 us (7%)
  local copies, waits for them, and re-layouts  43.4 us (6%)
  starting transfers between devices  22 us (3%)
  between operations  14.5 us (2%)
  other arithmetic  7.29 us (1%)
    psum x1, waiting for transfers between devices, body(): group_grad = lax.psum(kernel_part, ('rows', 'chan'))  291 us
    reduce_scatter x1, waiting for transfers between devices, body(): lax.psum_scatter(input_terms.reshape(rows_here, cols_here, input_terms.sh...  59.3 us
    reduce_scatter x1, waiting for transfers between devices, body(): lax.psum_scatter(third_total, 'chan', scatter_dimension=0, tiled=True)  44.5 us
    reduce_scatter x1, waiting for transfers between devices, body(): lax.psum_scatter(first_total, 'chan', scatter_dimension=0, tiled=True)  40 us
    all_gather x1, blocking collectives, body(): lax.all_gather(third_weight, 'chan', axis=0, tiled=True)  39.6 us
    all_gather x1, blocking collectives, body(): lax.all_gather(first_weight, 'chan', axis=0, tiled=True)  36.9 us
    conv_general_dilated x2, matrix products, group_conv(): lax.conv_general_dilated(padded[None], kernel, (1, 1), 'VALID', dimension...  23.3 us
    ppermute x4, waiting for transfers between devices, extended(): lax.ppermute(lax.slice_in_dim(block, 0, width, axis=dim), axis, backward)  21.5 us
  transfers between devices with their start and end apart: 16, of which 12 were waited for; matrix products, arithmetic and copies ran while one was open for 13% of the time, Pallas kernels for 0%

commit v1 on v0

--- a/solution.py
+++ b/solution.py
@@ -124,7 +124,8 @@
         tiled=True,
     ).astype(jnp.float32)
     images_grad = out_grad.astype(jnp.float32) + back_images
-    group_grad = lax.psum(kernel_part, ("rows", "chan"))
+    one_axis = lax.psum(kernel_part, "rows")
+    group_grad = lax.psum(one_axis, "chan")
     first_total, third_total = lax.psum((first_part, third_part), "rows")
     first_grad, third_grad = (
         lax.psum_scatter(first_total, "chan", scatter_dimension=0, tiled=True),

time: 701 us -> 493 us (0.70)
  waiting for transfers between devices: 487 us -> 283 us
    psum x1, waiting for transfers between devices: 291 us -> 78.4 us  [body(): group_grad = lax.psum(one_axis, 'chan')]
    psum x1, waiting for transfers between devices: 21.3 us -> 44.1 us  [body(): first_total, third_total = lax.psum((first_part, third_part), 'rows')]
    reduce_scatter x1, waiting for transfers between devices: 40 us -> 25.5 us  [body(): lax.psum_scatter(first_total, 'chan', scatter_dimension=0, tiled=True)]
  transfers between devices with their start and end apart: 16 -> 16, of which waited for: 12 -> 12; matrix products, arithmetic and copies ran while one was open for 13% -> 18% of each run, Pallas kernels for 0% -> 0%
where the time goes in v1:
time: 493 us; the launch traced here: 489 us
  waiting for transfers between devices  283 us (57%)
  blocking collectives  76.5 us (16%)
  matrix products  49 us (10%)
  local copies, waits for them, and re-layouts  37.7 us (8%)
  starting transfers between devices  22 us (4%)
  between operations  14.6 us (3%)
  other arithmetic  6.36 us (1%)
    psum x1, waiting for transfers between devices, body(): group_grad = lax.psum(one_axis, 'chan')  78.4 us
    reduce_scatter x1, waiting for transfers between devices, body(): lax.psum_scatter(input_terms.reshape(rows_here, cols_here, input_terms.sh...  59.7 us
    reduce_scatter x1, waiting for transfers between devices, body(): lax.psum_scatter(third_total, 'chan', scatter_dimension=0, tiled=True)  44.3 us
    psum x1, waiting for transfers between devices, body(): first_total, third_total = lax.psum((first_part, third_part), 'rows')  44.1 us
    all_gather x1, blocking collectives, body(): lax.all_gather(third_weight, 'chan', axis=0, tiled=True)  39.6 us
    all_gather x1, blocking collectives, body(): lax.all_gather(first_weight, 'chan', axis=0, tiled=True)  36.9 us
    reduce_scatter x1, waiting for transfers between devices, body(): lax.psum_scatter(first_total, 'chan', scatter_dimension=0, tiled=True)  25.5 us
    conv_general_dilated x2, matrix products, group_conv(): lax.conv_general_dilated(padded[None], kernel, (1, 1), 'VALID', dimension...  23.3 us
  transfers between devices with their start and end apart: 16, of which 12 were waited for; matrix products, arithmetic and copies ran while one was open for 18% of the time, Pallas kernels for 0%

profile of v1, /device:TPU:32, one launch (start us, length us, event | category | flops | bytes accessed | tf_op | source)
XLA Modules:
  0.0 489.4 jit_solution(568401535661509054)
XLA Ops:
  7.9 39.6 %all_gather.15 = bf16[1024,256]{1,0:T(8,128)(2,1)S(1)} all-gather(bf16[128,256]{1,0:T(8,128)(2,1)} %param.8), channel_id=1, replica_groups=mesh['rows'=4,'chan'=8,'filt'=8] {'chan'}, dimensions={0}, use_global_device_ids=true | all-gather | bytes 589824 | tf_op jit(solution)/shard_map/all_gather | solution.py:72
  47.5 3.8 fusion.10
  52.2 36.9 %all_gather.13 = bf16[2048,128]{1,0:T(8,128)(2,1)S(1)} all-gather(bf16[256,128]{1,0:T(8,128)(2,1)S(1)} %copy-done.17), channel_id=1, replica_groups=mesh['rows'=4,'chan'=8,'filt'=8] {'chan'}, dimensions={0}, use_global_device_ids=true | all-gather | bytes 589824 | tf_op jit(solution)/shard_map/all_gather | solution.py:71
  89.1 4.4 multiply_convert_fusion.3
  93.5 2.9 collective-permute-start
  96.4 1.3 collective-permute-start.1
  98.4 4.2 collective-permute-done.1
  103.2 3.4 collective-permute-start.2
  106.6 3.2 collective-permute-start.3
  109.8 0.9 shard_map.94
  110.7 8.0 %collective-permute-done.2 = bf16[6,1,128]{1,2,0:T(8,128)(2,1)S(1)} collective-permute-done((bf16[6,1,128]{1,2,0:T(8,128)(2,1)S(1)}, bf16[6,1,128]{1,2,0:T(8,128)(2,1)S(1)}, u32[]{:S(2)}, u32[]{:S(2)}) %collective-permute-start.2) | collective-permute-done | bytes 1568 | tf_op jit(solution)/shard_map/ppermute | solution.py:12
  118.7 10.6 %collective-permute-done.3 = bf16[6,1,128]{1,2,0:T(8,128)(2,1)S(1)} collective-permute-done((bf16[6,1,128]{1,2,0:T(8,128)(2,1)S(1)}, bf16[6,1,128]{1,2,0:T(8,128)(2,1)S(1)}, u32[]{:S(2)}, u32[]{:S(2)}) %collective-permute-start.3) | collective-permute-done | bytes 1568 | tf_op jit(solution)/shard_map/ppermute | solution.py:15
  130.0 5.8 %copy.36 = bf16[1,6,258,4,32]{4,0,3,2,1:T(2,128)(2,1)} copy(bf16[1,6,258,4,32]{2,4,3,1,0:T(8,128)(2,1)S(1)} %bitcast.121) | data formatting | bytes 792576 | tf_op jit(solution)/shard_map/broadcast_in_dim | solution.py:27
  135.8 9.4 %fusion.13 = f32[1,4,256,4,32]{4,0,3,2,1:T(1,128)S(1)} fusion(bf16[1,6,258,4,32]{4,0,3,2,1:T(2,128)(2,1)} %copy.36, bf16[3,3,32,4,32]{4,3,2,1,0:T(4,128)(2,1)} %shard_map.94), kind=kOutput, calls=%fused_computation.39 | convolution fusion | flops 75497472 | bytes 994304 | tf_op jit(solution)/shard_map/conv_general_dilated | solution.py:26
  145.3 3.5 copy.38
  148.8 1.3 copy.40
  150.1 2.0 multiply_convert_fusion.1
  152.2 3.4 collective-permute-start.4
  155.6 1.3 collective-permute-start.5
  157.5 4.3 collective-permute-done.5
  161.8 3.3 collective-permute-start.6
  165.1 2.8 collective-permute-start.7
  168.3 0.9 rev.6
  169.2 2.3 collective-permute-done.7
  171.9 5.9 %copy.44 = bf16[1,6,258,4,32]{4,0,3,2,1:T(2,128)(2,1)} copy(bf16[1,6,258,4,32]{2,4,3,1,0:T(8,128)(2,1)S(1)} %bitcast.120) | data formatting | bytes 792576 | tf_op jit(solution)/shard_map/broadcast_in_dim | solution.py:27
  177.8 13.8 %convolution_reduce_fusion = f32[4,256,4,32]{3,2,1,0:T(4,128)S(1)} fusion(bf16[1,6,258,4,32]{4,0,3,2,1:T(2,128)(2,1)} %copy.44, bf16[3,3,32,4,32]{4,3,2,1,0:T(4,128)(2,1)} %rev.6), kind=kOutput, calls=%fused_computation.2 | convolution fusion | flops 75497472 | bytes 994304 | tf_op jit(solution)/shard_map/conv_general_dilated | solution.py:26
  191.7 1.7 reshape.99
  193.3 1.4 multiply_convert_fusion
  194.8 3.9 convolution_bitcast_fusion
  200.7 0.9 copy.48
  201.6 1.8 reshape.85
  203.6 0.9 reshape.88
  204.7 0.9 reshape.89
  207.9 3.3 convolution_bitcast_fusion.1
  212.4 1.2 fusion.6
  214.0 1.2 fusion.3
  216.0 0.9 reshape.95
  216.9 25.5 %reduce-scatter.9.cloned.1.call-done = f32[256,128]{0,1:T(8,128)} async-done(((f32[2048,128]{0,1:T(8,128)}), f32[256,128]{0,1:T(8,128)}) %reduce-scatter.9.cloned.1.call-update) | async-done | bytes 131088 | tf_op jit(solution)/shard_map/reduce_scatter | solution.py:131
  242.4 44.3 %reduce-scatter.11.cloned.1.call-done = f32[128,256]{1,0:T(8,128)} async-done(((f32[1024,256]{1,0:T(8,128)}), f32[128,256]{1,0:T(8,128)}) %reduce-scatter.11.cloned.1.call-update) | async-done | bytes 131088 | tf_op jit(solution)/shard_map/reduce_scatter | solution.py:132
  286.8 3.2 convolution_convert_fusion
  290.1 1.0 copy-done.10
  291.1 3.1 fusion
  294.2 44.1 %all-reduce.6.cloned.1.call-done = (f32[256,128]{0,1:T(8,128)}, f32[3,3,32,128]{3,2,1,0:T(8,128)}, f32[128,256]{1,0:T(8,128)}) async-done(((f32[256,128]{0,1:T(8,128)}, f32[3,3,32,128]{3,2,1,0:T(8,128)}, f32[128,256]{1,0:T(8,128)}), (f32[256,128]{0,1:T(8,128)}, f32[3,3,32,128]{3,2,1,0:T(8,128)}, f32[128,256]{1,0:T(8,128)})) %all-reduce.6.cloned.1.call-update) | async-done | bytes 409616 | tf_op jit(solution)/shard_map/psum | solution.py:129
  338.4 1.7 copy.60
  340.1 59.7 %reduce-scatter.7.cloned.1.call-done = bf16[4,256,256]{2,1,0:T(8,128)(2,1)} async-done(((bf16[4,256,2048]{2,1,0:T(8,128)(2,1)}), bf16[4,256,256]{2,1,0:T(8,128)(2,1)}) %reduce-scatter.7.cloned.1.call-update) | async-done | bytes 524304 | tf_op jit(solution)/shard_map/reduce_scatter | solution.py:120
  399.8 2.1 convert_add_fusion
  401.9 78.4 %all-reduce.4.cloned.1.call-done = f32[3,3,32,128]{3,2,1,0:T(8,128)} async-done(((f32[3,3,32,128]{3,2,1,0:T(8,128)}), f32[3,3,32,128]{3,2,1,0:T(8,128)}) %all-reduce.4.cloned.1.call-update) | async-done | bytes 147472 | tf_op jit(solution)/shard_map/psum | solution.py:128
  480.3 1.6 copy.79
  (98 shorter events, 12.8 us)
Async XLA Ops:
  7.2 81.9 %all-gather.3.cloned.1.call-start = ((), (), s32[]{:S(2)}) async-start(), calls=%async_computation.4 | async-start | bytes 4718592 | tf_op jit(solution)/shard_map/all_gather | solution.py:76
  7.9 142.2 %reduce-scatter.5.cloned.1.call-start = ((), (), s32[]{:S(2)}) async-start(), calls=%async_computation.6 | async-start | bytes 4718592 | tf_op jit(solution)/shard_map/reduce_scatter | solution.py:96
  51.3 0.8 copy-start.17
  51.4 156.5 %all-gather.5.cloned.1.call-start = ((), (), s32[]{:S(2)}) async-start(), calls=%async_computation.5 | async-start | bytes 2359296 | tf_op jit(solution)/shard_map/all_gather | solution.py:87
  89.1 4.4 copy-start
  93.5 16.2 %copy-start.16 = (bf16[3,3,32,128]{3,2,1,0:T(8,128)(2,1)S(1)}, bf16[3,3,32,128]{3,2,1,0:T(8,128)(2,1)}, u32[]{:S(2)}) copy-start(bf16[3,3,32,128]{3,2,1,0:T(8,128)(2,1)} %param.7) | copy-start | bytes 221188
  93.5 4.8 collective-permute-start
  96.4 6.2 %collective-permute-start.1 = (bf16[1,256,128]{2,1,0:T(8,128)(2,1)S(1)}, bf16[1,256,128]{2,1,0:T(8,128)(2,1)S(1)}, u32[]{:S(2)}, u32[]{:S(2)}) collective-permute-start(bf16[1,256,128]{2,1,0:T(8,128)(2,1)S(1)} %get-tuple-element.37), channel_id=1, source_target_pairs={{64,0},{128,64},{192,128},{65,1},{129,65},{193,129},{66,2},{130,66... | collective-permute-start | bytes 196616 | tf_op jit(solution)/shard_map/ppermute | solution.py:15
  98.3 4.6 copy-start.11
  102.6 0.6 copy-start.13
  103.2 15.5 %collective-permute-start.2 = (bf16[6,1,128]{1,2,0:T(8,128)(2,1)S(1)}, bf16[6,1,128]{1,2,0:T(8,128)(2,1)S(1)}, u32[]{:S(2)}, u32[]{:S(2)}) collective-permute-start(bf16[6,1,128]{1,2,0:T(8,128)(2,1)S(1)} %get-tuple-element.30), channel_id=1, source_target_pairs={{0,8},{8,16},{16,24},{24,32},{32,40},{40,48},{48,56},{1,9},{9,17},... | collective-permute-start | bytes 4616 | tf_op jit(solution)/shard_map/ppermute | solution.py:12
  106.6 22.7 %collective-permute-start.3 = (bf16[6,1,128]{1,2,0:T(8,128)(2,1)S(1)}, bf16[6,1,128]{1,2,0:T(8,128)(2,1)S(1)}, u32[]{:S(2)}, u32[]{:S(2)}) collective-permute-start(bf16[6,1,128]{1,2,0:T(8,128)(2,1)S(1)} %get-tuple-element.31), channel_id=1, source_target_pairs={{8,0},{16,8},{24,16},{32,24},{40,32},{48,40},{56,48},{9,1},{17,9},... | collective-permute-start | bytes 4616 | tf_op jit(solution)/shard_map/ppermute | solution.py:15
  118.7 17.1 %copy-start.6 = (bf16[6,1,128]{1,2,0:T(8,128)(2,1)}, bf16[6,1,128]{1,2,0:T(8,128)(2,1)S(1)}, u32[]{:S(2)}) copy-start(bf16[6,1,128]{1,2,0:T(8,128)(2,1)S(1)} %collective-permute-done.2) | copy-start | bytes 4612
  129.3 0.7 copy-start.8
  148.8 19.0 %copy-start.3 = (bf16[3,3,32,4,32]{4,3,2,1,0:T(4,128)(2,1)S(1)}, bf16[3,3,32,4,32]{4,3,2,1,0:T(4,128)(2,1)}, u32[]{:S(2)}) copy-start(bf16[3,3,32,4,32]{4,3,2,1,0:T(4,128)(2,1)} %shard_map.94) | copy-start | bytes 221188
  152.2 90.3 %reduce-scatter.9.cloned.1.call-start = ((), (), s32[]{:S(2)}) async-start(), calls=%async_computation.9 | async-start | bytes 1179648 | tf_op jit(solution)/shard_map/reduce_scatter | solution.py:131
  152.2 5.3 %collective-permute-start.4 = (bf16[1,256,128]{2,1,0:T(8,128)(2,1)S(1)}, bf16[1,256,128]{2,1,0:T(8,128)(2,1)S(1)}, u32[]{:S(2)}, u32[]{:S(2)}) collective-permute-start(bf16[1,256,128]{2,1,0:T(8,128)(2,1)S(1)} %get-tuple-element.34), channel_id=1, source_target_pairs={{0,64},{64,128},{128,192},{1,65},{65,129},{129,193},{2,66},{66,130... | collective-permute-start | bytes 196616 | tf_op jit(solution)/shard_map/ppermute | solution.py:12
  155.6 6.2 %collective-permute-start.5 = (bf16[1,256,128]{2,1,0:T(8,128)(2,1)S(1)}, bf16[1,256,128]{2,1,0:T(8,128)(2,1)S(1)}, u32[]{:S(2)}, u32[]{:S(2)}) collective-permute-start(bf16[1,256,128]{2,1,0:T(8,128)(2,1)S(1)} %get-tuple-element.35), channel_id=1, source_target_pairs={{64,0},{128,64},{192,128},{65,1},{129,65},{193,129},{66,2},{130,66... | collective-permute-start | bytes 196616 | tf_op jit(solution)/shard_map/ppermute | solution.py:15
  161.8 7.4 %collective-permute-start.6 = (bf16[6,1,128]{2,1,0:T(2,128)(2,1)S(1)}, bf16[6,1,128]{2,1,0:T(2,128)(2,1)S(1)}, u32[]{:S(2)}, u32[]{:S(2)}) collective-permute-start(bf16[6,1,128]{2,1,0:T(2,128)(2,1)S(1)} %get-tuple-element.28), channel_id=1, source_target_pairs={{0,8},{8,16},{16,24},{24,32},{32,40},{40,48},{48,56},{1,9},{9,17},... | collective-permute-start | bytes 4616 | tf_op jit(solution)/shard_map/ppermute | solution.py:12
  165.1 6.4 %collective-permute-start.7 = (bf16[6,1,128]{2,1,0:T(2,128)(2,1)S(1)}, bf16[6,1,128]{2,1,0:T(2,128)(2,1)S(1)}, u32[]{:S(2)}, u32[]{:S(2)}) collective-permute-start(bf16[6,1,128]{2,1,0:T(2,128)(2,1)S(1)} %get-tuple-element.29), channel_id=1, source_target_pairs={{8,0},{16,8},{24,16},{32,24},{40,32},{48,40},{56,48},{9,1},{17,9},... | collective-permute-start | bytes 4616 | tf_op jit(solution)/shard_map/ppermute | solution.py:15
  194.7 4.5 copy-start.12
  194.7 4.5 copy-start.14
  198.7 1.3 copy-start.7
  198.7 1.3 copy-start.9
  198.7 88.0 %reduce-scatter.11.cloned.1.call-start = ((), (), s32[]{:S(2)}) async-start(), calls=%async_computation.10 | async-start | bytes 1179648 | tf_op jit(solution)/shard_map/reduce_scatter | solution.py:132
  205.6 2.3 copy-start.2
  207.8 3.5 copy-start.5
  211.2 0.9 copy-start.4
  211.2 127.1 %all-reduce.6.cloned.1.call-start = ((), (), s32[]{:S(2)}) async-start(), calls=%async_computation.11 | async-start | bytes 819200 | tf_op jit(solution)/shard_map/psum | solution.py:129
  213.9 72.9 %copy-start.1 = (bf16[2048,128]{1,0:T(8,128)(2,1)S(1)}, bf16[2048,128]{1,0:T(8,128)(2,1)}, u32[]{:S(2)}) copy-start(bf16[2048,128]{1,0:T(8,128)(2,1)} %copy-done) | copy-start | bytes 1572868
  286.8 113.0 %reduce-scatter.7.cloned.1.call-start = ((), (), s32[]{:S(2)}) async-start(), calls=%async_computation.7 | async-start | bytes 4718592 | tf_op jit(solution)/shard_map/reduce_scatter | solution.py:120
  290.1 1.0 copy-start.10
  290.1 190.2 %all-reduce.4.cloned.1.call-start = ((), (), s32[]{:S(2)}) async-start(), calls=%async_computation.8 | async-start | bytes 294912 | tf_op jit(solution)/shard_map/psum | solution.py:128
  338.4 143.5 %copy-start.15 = (f32[128,256]{1,0:T(8,128)S(1)}, f32[128,256]{1,0:T(8,128)}, u32[]{:S(2)}) copy-start(f32[128,256]{1,0:T(8,128)} %get-tuple-element.47) | copy-start | bytes 393220
Sparse Core Ops, SparseCore 0:
  9.8 60.3 all-gather.2
  72.7 76.6 reduce-scatter.4
  152.3 42.8 all-gather.4
  198.9 43.5 reduce-scatter.8
  244.8 41.9 reduce-scatter.10
  289.7 48.5 all-reduce.5
  341.1 58.7 reduce-scatter.6
  402.6 77.6 all-reduce.3
